TPU v7x, 32 devices: a whole 2x2x4 slice. The times are simulated.
32 devices in a mesh: dp: 8 (over y, x, core), ind: 4 (over z).
Axes of the slice: x: 2, y: 2, z: 4, core: 2. Of those that a mesh axis runs over, the one named last changes fastest.
Arguments:
- x_points: float32 [3, 16384], P(None, 'dp'), may hold values from 0 to 1
- z_points: float32 [3, 16384], P(None, 'ind'), may hold values from 0 to 1
- length_scales: float32 [3], replicated, may hold values from 0.35 to 0.7
- dpsi_grad: float32 [16384, 16384], P('dp', 'ind'), may hold values from -0.625 to 0.625
- block_rows: int32 [8, 4, 6], P('dp', 'ind'), may hold values from 0 to 7, as said below
- block_cols: int32 [8, 4, 6], P('dp', 'ind'), may hold values from 0 to 15, as said below
- block_count: int32 [8, 4], P('dp', 'ind'), may hold values from 3 to 6, as said below
Outputs:
- dk_blocks: float32 [8, 4, 6, 256, 256], P('dp', 'ind')
- z_grad: float32 [3, 16384], P(None, 'ind')
- scale_grad: float32 [3], replicated
Inputs may be any that keep to these rules, and one draw needn't show every extreme that they name: `block_rows`: within a tile the live slots lie in distinct row blocks, and the live slots of all tiles of one row group lie in at most 6 distinct row blocks; entries of unused slots carry no meaning. `block_cols`: entries of unused slots carry no meaning. `block_count`: some tile holds exactly 6 listed blocks in every draw.
All inputs are finite; a program needn't handle non-finite values.
Results may differ from a plain program's by a relative error of at most 0.0003.
Values sent between devices are 32-bit elements; how exact they have to be, the bound alone decides.
A program may use at most 128 MiB of HBM per device.

v0:
```python
import jax
import jax.numpy as jnp
from jax import lax
from jax.sharding import PartitionSpec as P

M = 16384
BS = 256


def wendland(x_rows, z_cols, length_scales):
    dist_sq = jnp.zeros((x_rows.shape[1], z_cols.shape[1]), x_rows.dtype)
    for dim_q in range(x_rows.shape[0]):
        offset = (x_rows[dim_q][:, None] - z_cols[dim_q][None, :]) / length_scales[dim_q]
        dist_sq = dist_sq + offset * offset
    radius = jnp.sqrt(dist_sq)
    remain = jnp.maximum(1.0 - radius, 0.0)
    remain_cube = remain * remain * remain
    return (remain_cube * remain * (4.0 * radius + 1.0), -10.0 * remain_cube)


def on_device(x_points, z_points, length_scales, dpsi_grad, block_rows, block_cols, block_count):
    highest = lax.Precision.HIGHEST
    groups_dp = lax.axis_size("dp")
    groups_ind = lax.axis_size("ind")
    dp_index = lax.axis_index("dp")
    ind_index = lax.axis_index("ind")
    owner_ratio = groups_dp // groups_ind
    col_blocks = M // (BS * groups_ind)
    own_blocks = M // (BS * groups_dp)
    dim_count = x_points.shape[0]
    slot_count = block_rows.shape[2]
    row_count = x_points.shape[1] // BS
    slot_ids = jnp.arange(slot_count, dtype=jnp.int32)
    batched_kernel = jax.vmap(wendland, in_axes=(0, 0, None))
    all_rows, all_cols, all_count = (
        lax.all_gather(block_rows, ("dp", "ind"), axis=0, tiled=True),
        lax.all_gather(block_cols, ("dp", "ind"), axis=0, tiled=True),
        lax.all_gather(block_count, ("dp", "ind"), axis=0, tiled=True),
    )
    all_rows = all_rows.reshape(groups_dp, groups_ind, slot_count)
    all_cols = all_cols.reshape(groups_dp, groups_ind, slot_count)
    all_count = all_count.reshape(groups_dp, groups_ind)
    live_all = slot_ids[None, None, :] < all_count[:, :, None]
    z_all = lax.all_gather(z_points, "ind", axis=1, tiled=True)
    z_blocks = z_all.reshape(dim_count, M // BS, BS)
    own_rows = block_rows[0, 0]
    own_cols = block_cols[0, 0]
    own_live = (slot_ids < block_count[0, 0]).astype(jnp.float32)
    x_own = jnp.transpose(x_points.reshape(dim_count, row_count, BS)[:, own_rows, :], (1, 0, 2))
    my_group = dp_index // owner_ratio
    my_part = dp_index % owner_ratio
    dest_rows = all_rows[:, ind_index, :]
    dest_cols = all_cols[:, ind_index, :]
    source_rows = all_rows[:, my_group, :]
    source_cols = all_cols[:, my_group, :]
    source_live = live_all[:, my_group, :]
    matched = source_live[:, None, :] & (source_rows[:, None, :] == dest_rows[:, :, None])
    found_col = jnp.sum(jnp.where(matched, source_cols[:, None, :], 0), axis=2)
    keep_weight = (jnp.any(matched, axis=2) & (found_col // own_blocks == my_part)).astype(
        jnp.float32
    )
    row_start = (found_col - my_part * own_blocks) * BS
    col_start = dest_cols * BS

    def pick_tile(row_at, col_at, weight):
        return lax.dynamic_slice(dpsi_grad, (row_at, col_at), (BS, BS)) * weight

    outgoing = jax.vmap(pick_tile)(
        row_start.reshape(-1), col_start.reshape(-1), keep_weight.reshape(-1)
    )
    outgoing = outgoing.reshape(groups_dp, slot_count, BS, BS)
    received = lax.all_to_all(outgoing, "dp", split_axis=0, concat_axis=0, tiled=True)
    grouped = jnp.sum(received.reshape(groups_ind, owner_ratio, slot_count, BS, BS), axis=1)
    row_tiles = all_rows[dp_index]
    col_tiles = all_cols[dp_index]
    live_tiles = live_all[dp_index]
    near_match = live_tiles[None, :, :] & (row_tiles[None, :, :] == own_rows[:, None, None])
    near_weight = jnp.any(near_match, axis=2).astype(jnp.float32)
    near_local = jnp.sum(jnp.where(near_match, col_tiles[None, :, :], 0), axis=2)
    near_blocks = jnp.arange(groups_ind, dtype=jnp.int32)[None, :] * col_blocks + near_local
    z_near = jnp.transpose(z_blocks[:, near_blocks, :], (1, 0, 2, 3)).reshape(
        slot_count, dim_count, groups_ind * BS
    )
    kernel, _ = batched_kernel(x_own, z_near, length_scales)
    masked = kernel * jnp.repeat(near_weight, BS, axis=1)[:, None, :]
    dk_local = jnp.einsum(
        "spgk,gskc->spc", masked.reshape(slot_count, BS, groups_ind, BS), grouped, precision=highest
    )
    dk_local = dk_local * own_live[:, None, None]
    z_own = jnp.transpose(z_points.reshape(dim_count, col_blocks, BS)[:, own_cols, :], (1, 0, 2))
    _, slopes = batched_kernel(x_own, z_own, length_scales)
    grad_k = dk_local * slopes
    col_sum = jnp.sum(grad_k, axis=1)
    x_weighted = jnp.einsum("sqn,snm->sqm", x_own, grad_k, precision=highest)
    inverse_square = -2.0 / (length_scales * length_scales)
    z_parts = inverse_square[None, :, None] * (x_weighted - z_own * col_sum[:, None, :])
    scale_terms = []
    for dim_q in range(dim_count):
        offset = x_own[:, dim_q, :, None] - z_own[:, dim_q, None, :]
        scale_terms.append(jnp.sum(grad_k * offset * offset, axis=(1, 2)))
    cube_scale = length_scales * length_scales * length_scales
    scale_parts = (-2.0 / cube_scale)[None, :] * jnp.stack(scale_terms, axis=1)
    onehot = (own_cols[:, None] == jnp.arange(col_blocks, dtype=jnp.int32)[None, :]).astype(
        jnp.float32
    )
    z_local = jnp.einsum("tc,tqb->qcb", onehot, z_parts, precision=highest).reshape(
        dim_count, col_blocks * BS
    )
    scale_local = jnp.sum(scale_parts, axis=0)
    z_grad = lax.psum(z_local, "dp")
    scale_grad = lax.psum(scale_local, ("dp", "ind"))
    return (dk_local.reshape(1, 1, slot_count, BS, BS), z_grad, scale_grad)


def solution(mesh):
    return jax.shard_map(
        on_device,
        mesh=mesh,
        in_specs=(
            P(None, "dp"),
            P(None, "ind"),
            P(),
            P("dp", "ind"),
            P("dp", "ind", None),
            P("dp", "ind", None),
            P("dp", "ind"),
        ),
        out_specs=(P("dp", "ind", None, None, None), P(None, "ind"), P()),
        check_vma=False,
    )
```

profile of v0, /device:TPU:0, one launch (start us, length us, event | category | flops | bytes accessed | tf_op | source)
XLA Modules:
  0.0 603.4 jit_solution(6014188086941941241)
XLA Ops:
  0.7 69.5 %all_gather.14 = s32[32,1,6]{2,1,0:T(1,128)S(1)} all-gather(s32[1,1,6]{2,1,0:T(1,128)} %param.11), channel_id=1, replica_groups=mesh['dp'=8,'ind'=4] {'dp','ind'}, dimensions={0}, use_global_device_ids=true | all-gather | bytes 792 | tf_op jit(solution)/shard_map/all_gather | solution.py:36
  71.0 36.8 %all-reduce = s32[32]{0:T(128)S(1)} all-reduce(s32[32]{0:T(128)S(1)} %bitcast_dynamic-update-slice_fusion.1), channel_id=1, replica_groups=mesh['dp'=8,'ind'=4] {'dp','ind'}, use_global_device_ids=true, to_apply=%add | all-reduce | flops 32 | bytes 256
  108.1 66.0 %all_gather.15 = s32[32,1,6]{2,1,0:T(1,128)S(1)} all-gather(s32[1,1,6]{2,1,0:T(1,128)} %param.12), channel_id=1, replica_groups=mesh['dp'=8,'ind'=4] {'dp','ind'}, dimensions={0}, use_global_device_ids=true | all-gather | bytes 792 | tf_op jit(solution)/shard_map/all_gather | solution.py:37
  175.1 185.1 %while.1 = (s32[]{:T(128)}, f32[2048,4096]{1,0:T(8,128)}, s32[48,2]{0,1:T(2,128)S(1)}, f32[48,256,256]{2,1,0:T(8,128)}, s32[]{:T(128)}) while((s32[]{:T(128)}, f32[2048,4096]{1,0:T(8,128)}, s32[48,2]{0,1:T(2,128)S(1)}, f32[48,256,256]{2,1,0:T(8,128)}, s32[]{:T(128)}) %tuple.43), condition=%wide.while_cond, body=%wide.while_body.sunk | while | flops 2 | bytes 525921 | solution.py:66
  183.5 3.2 bitcast_dynamic-update-slice_fusion.3
  210.5 3.2 bitcast_dynamic-update-slice_fusion.3
  252.8 3.2 bitcast_dynamic-update-slice_fusion.3
  256.7 3.2 bitcast_dynamic-update-slice_fusion.3
  260.6 3.2 bitcast_dynamic-update-slice_fusion.3
  276.0 3.2 bitcast_dynamic-update-slice_fusion.3
  279.9 3.2 bitcast_dynamic-update-slice_fusion.3
  283.8 3.2 bitcast_dynamic-update-slice_fusion.3
  310.7 3.2 bitcast_dynamic-update-slice_fusion.3
  318.5 3.2 bitcast_dynamic-update-slice_fusion.3
  341.6 3.2 bitcast_dynamic-update-slice_fusion.3
  357.0 3.2 bitcast_dynamic-update-slice_fusion.3
  360.3 11.3 %broadcast_multiply_fusion = f32[8,6,256,256]{3,2,1,0:T(8,128)} fusion(f32[8,6,256,256]{3,2,1,0:T(8,128)} %bitcast.100, f32[8,6]{1,0:T(8,128)S(1)} %copy.51), kind=kLoop, calls=%fused_computation.11 | loop fusion | flops 3145728 | bytes 25166016 | tf_op jit(solution)/shard_map/vmap()/mul | solution.py:66
  371.7 5.5 all-to-all-start
  377.9 14.4 %all_gather.12 = f32[3,16384]{1,0:T(4,128)S(1)} all-gather(f32[3,4096]{1,0:T(4,128)S(1)} %copy-done.2), channel_id=1, replica_groups=mesh['dp'=8,'ind'=4] {'ind'}, dimensions={1}, use_global_device_ids=true | all-gather | bytes 245760 | tf_op jit(solution)/shard_map/all_gather | solution.py:44
  395.3 120.9 %all-to-all-done = f32[8,6,256,256]{3,2,1,0:T(8,128)} async-done(((f32[8,6,256,256]{3,2,1,0:T(8,128)}), f32[8,6,256,256]{3,2,1,0:T(8,128)}, u32[]{:S(2)}, u32[]{:S(2)}) %all-to-all-start) | async-done | bytes 12582944 | tf_op jit(solution)/shard_map/all_to_all | solution.py:72
  516.2 6.6 %bitcast_reduce_fusion = f32[4,6,256,256]{3,2,1,0:T(8,128)S(1)} fusion(f32[8,6,256,256]{3,2,1,0:T(8,128)} %all-to-all-done), kind=kLoop, calls=%fused_computation.5 | loop fusion | flops 1572864 | bytes 18874368 | tf_op jit(solution)/shard_map/reduce_sum | solution.py:73
  522.8 16.3 %fusion.44 = (f32[6]{0:T(128)S(1)}, f32[6]{0:T(128)S(1)}, f32[6]{0:T(128)S(1)}, f32[6,256]{1,0:T(8,128)S(1)}, f32[6,256,256]{2,1,0:T(8,128)}, /*index=5*/f32[6,256,256]{2,1,0:T(8,128)}) fusion(f32[6,256]{1,0:T(8,128)S(1)} %get-tuple-element.51, f32[6,256]{1,0:T(8,128)S(1)} %get-tuple-element.52, f32[6,256]{1,0:T(8,128)S(1)} %get-tuple-element.47, ...), kind=kOutput, calls=%fused_computation.61 | convolution fusion | flops 4874304000 | bytes 9554124 | tf_op jit(solution)/shard_map/spgk,gskc->spc/dot_general | solution.py:86
  539.3 37.2 %psum.15 = f32[3]{0:T(128)} all-reduce(f32[3]{0:T(128)S(1)} %fusion.60), channel_id=1, replica_groups=mesh['dp'=8,'ind'=4] {'dp','ind'}, use_global_device_ids=true, to_apply=%region_11.12 | all-reduce | flops 3 | bytes 24 | tf_op jit(solution)/shard_map/psum | solution.py:111
  579.1 24.3 %psum.14 = f32[3,4096]{1,0:T(4,128)} all-reduce(f32[3,4096]{1,0:T(4,128)S(1)} %bitcast.103), channel_id=1, replica_groups=mesh['dp'=8,'ind'=4] {'dp'}, use_global_device_ids=true, to_apply=%region_6.7 | all-reduce | flops 12288 | bytes 98304 | tf_op jit(solution)/shard_map/psum | solution.py:110
  (205 shorter events, 154.4 us)
Async XLA Ops:
  0.6 393.4 %copy-start = (f32[3,2048]{1,0:T(4,128)S(1)}, f32[3,2048]{1,0:T(4,128)}, u32[]{:S(2)}) copy-start(f32[3,2048]{1,0:T(4,128)} %param.7) | copy-start | bytes 73732
  371.7 5.6 copy-start.4
  371.7 6.2 %copy-start.2 = (f32[3,4096]{1,0:T(4,128)S(1)}, f32[3,4096]{1,0:T(4,128)}, u32[]{:S(2)}) copy-start(f32[3,4096]{1,0:T(4,128)} %param.8) | copy-start | bytes 147460
  371.7 21.7 %copy-start.5 = (s32[1,1,6]{2,1,0:T(1,128)S(1)}, s32[1,1,6]{2,1,0:T(1,128)}, u32[]{:S(2)}) copy-start(s32[1,1,6]{2,1,0:T(1,128)} %param.12) | copy-start | bytes 76
  371.7 22.9 %copy-start.3 = (f32[3]{0:T(128)S(1)}, f32[3]{0:T(128)}, u32[]{:S(2)}) copy-start(f32[3]{0:T(128)} %param.9) | copy-start | bytes 40
  371.7 144.5 %all-to-all-start = ((f32[8,6,256,256]{3,2,1,0:T(8,128)}), f32[8,6,256,256]{3,2,1,0:T(8,128)}, u32[]{:S(2)}, u32[]{:S(2)}) async-start(f32[8,6,256,256]{3,2,1,0:T(8,128)} %broadcast_multiply_fusion), calls=%async_computation | async-start | bytes 25165824 | tf_op jit(solution)/shard_map/all_to_all | solution.py:72
  522.8 80.6 %copy-start.1 = (f32[3,2048]{1,0:T(4,128)S(1)}, f32[3,2048]{1,0:T(4,128)}, u32[]{:S(2)}) copy-start(f32[3,2048]{1,0:T(4,128)} %param.7) | copy-start | bytes 73732
where the time goes:
time: 607 us; the launch traced here: 603 us
  blocking collectives  248 us (41%)
  local copies, waits for them, and re-layouts  189 us (31%)
  waiting for transfers between devices  121 us (20%)
  other arithmetic  19.3 us (3%)
  matrix products  18.8 us (3%)
    gather x144, local copies, waits for them, and re-layouts  185 us
    all_to_all x1, waiting for transfers between devices, on_device(): lax.all_to_all(outgoing, 'dp', split_axis=0, concat_axis=0, tiled=True)  121 us
    all_gather x1, blocking collectives, on_device(): lax.all_gather(block_rows, ('dp', 'ind'), axis=0, tiled=True)  69.5 us
    all_gather x1, blocking collectives, on_device(): lax.all_gather(block_cols, ('dp', 'ind'), axis=0, tiled=True)  66 us
    psum x1, blocking collectives, on_device(): scale_grad = lax.psum(scale_local, ('dp', 'ind'))  37.2 us
    unnamed x1, blocking collectives  36.8 us
    psum x1, blocking collectives, on_device(): z_grad = lax.psum(z_local, 'dp')  24.3 us
    dot_general x1, matrix products, on_device(): jnp.einsum('spgk,gskc->spc', masked.reshape(slot_count, BS, groups_ind, B...  16.3 us
  transfers between devices with their start and end apart: 1, of which 1 were waited for; matrix products, arithmetic and copies ran while one was open for 1% of the time, Pallas kernels for 0%

commit v1 on v0

v1 whole, which is shorter than its diff:
```python
import functools

import jax
import jax.numpy as jnp
from jax import lax
from jax.experimental import pallas as pl
from jax.experimental.pallas import tpu as pltpu
from jax.sharding import PartitionSpec as P

M = 16384
BS = 256


def wendland(x_rows, z_cols, length_scales):
    dist_sq = jnp.zeros((x_rows.shape[1], z_cols.shape[1]), x_rows.dtype)
    for dim_q in range(x_rows.shape[0]):
        offset = (x_rows[dim_q][:, None] - z_cols[dim_q][None, :]) / length_scales[dim_q]
        dist_sq = dist_sq + offset * offset
    radius = jnp.sqrt(dist_sq)
    remain = jnp.maximum(1.0 - radius, 0.0)
    remain_cube = remain * remain * remain
    return (remain_cube * remain * (4.0 * radius + 1.0), -10.0 * remain_cube)


def peers_of(axis, stride):
    size = lax.axis_size(axis) // stride
    index = lax.axis_index(axis)
    me = index // stride
    lane = index % stride
    others = []
    for step in range(1, size):
        other = lax.rem(me + step, size)
        others.append((other, {axis: other * stride + lane}))
    return me, others


def exchange_kernel(axis, stride, same, in_ref, out_ref, send_sem, recv_sem, local_sem):
    me, others = peers_of(axis, stride)
    barrier = pltpu.get_barrier_semaphore()
    for _, target in others:
        pl.semaphore_signal(barrier, inc=1, device_id=target, device_id_type=pl.DeviceIdType.MESH)
    pl.semaphore_wait(barrier, len(others))
    copies = []
    for step, (other, target) in enumerate(others):
        copy = pltpu.make_async_remote_copy(
            src_ref=in_ref if same else in_ref.at[other],
            dst_ref=out_ref.at[me],
            send_sem=send_sem.at[step],
            recv_sem=recv_sem.at[step],
            device_id=target,
            device_id_type=pl.DeviceIdType.MESH,
        )
        copy.start()
        copies.append(copy)
    own = pltpu.make_async_copy(in_ref if same else in_ref.at[me], out_ref.at[me], local_sem)
    own.start()
    own.wait()
    for copy in copies:
        copy.wait()


def exchange(array, axis, collective_id, stride=1, same=True, space=pltpu.VMEM):
    size = lax.axis_size(axis) // stride
    shape = (size,) + array.shape if same else array.shape
    return pl.pallas_call(
        functools.partial(exchange_kernel, axis, stride, same),
        out_shape=jax.ShapeDtypeStruct(shape, array.dtype),
        in_specs=[pl.BlockSpec(memory_space=space)],
        out_specs=pl.BlockSpec(memory_space=space),
        scratch_shapes=[
            pltpu.SemaphoreType.DMA((size - 1,)),
            pltpu.SemaphoreType.DMA((size - 1,)),
            pltpu.SemaphoreType.DMA,
        ],
        compiler_params=pltpu.CompilerParams(collective_id=collective_id, has_side_effects=True),
    )(array)


def pick_kernel(row_ref, col_ref, keep_ref, in_ref, out_ref):
    keep = keep_ref[pl.program_id(0)] > 0

    @pl.when(keep)
    def _():
        out_ref[0] = in_ref[...]

    @pl.when(jnp.logical_not(keep))
    def _():
        out_ref[...] = jnp.zeros_like(out_ref)


def pick_tiles(dpsi_grad, row_blocks, col_blocks, keep):
    count = row_blocks.shape[0]
    return pl.pallas_call(
        pick_kernel,
        out_shape=jax.ShapeDtypeStruct((count, BS, BS), dpsi_grad.dtype),
        grid_spec=pltpu.PrefetchScalarGridSpec(
            num_scalar_prefetch=3,
            grid=(count,),
            in_specs=[pl.BlockSpec((BS, BS), lambda t, rows, cols, keeps: (rows[t], cols[t]))],
            out_specs=pl.BlockSpec((1, BS, BS), lambda t, rows, cols, keeps: (t, 0, 0)),
        ),
    )(row_blocks, col_blocks, keep, dpsi_grad)


def on_device(x_points, z_points, length_scales, dpsi_grad, block_rows, block_cols, block_count):
    highest = lax.Precision.HIGHEST
    groups_dp = lax.axis_size("dp")
    groups_ind = lax.axis_size("ind")
    dp_index = lax.axis_index("dp")
    ind_index = lax.axis_index("ind")
    owner_ratio = groups_dp // groups_ind
    col_blocks = M // (BS * groups_ind)
    own_blocks = M // (BS * groups_dp)
    dim_count = x_points.shape[0]
    slot_count = block_rows.shape[2]
    row_count = x_points.shape[1] // BS
    slot_ids = jnp.arange(slot_count, dtype=jnp.int32)
    batched_kernel = jax.vmap(wendland, in_axes=(0, 0, None))
    def lane_row(values):
        return jnp.pad(values, (0, 128 - values.shape[0]))[None, :]

    meta = jnp.pad(
        jnp.concatenate(
            [lane_row(block_rows[0, 0]), lane_row(block_cols[0, 0]), lane_row(block_count[0])]
        ),
        ((0, 5), (0, 0)),
    )
    meta_ind = exchange(meta, "ind", 0)
    z_all = exchange(z_points, "ind", 1)
    meta_all = exchange(meta_ind.reshape(groups_ind * 8, 128), "dp", 2)
    meta_all = meta_all.reshape(groups_dp, groups_ind, 8, 128)
    all_count = meta_all[:, :, 2, 0]
    live_all = slot_ids[None, None, :] < all_count[:, :, None]
    all_rows = jnp.where(live_all, meta_all[:, :, 0, :slot_count], 0)
    all_cols = jnp.where(live_all, meta_all[:, :, 1, :slot_count], 0)
    z_blocks = z_all.reshape(groups_ind, dim_count, col_blocks, BS)
    own_mask = slot_ids < block_count[0, 0]
    own_rows = jnp.where(own_mask, block_rows[0, 0], 0)
    own_cols = jnp.where(own_mask, block_cols[0, 0], 0)
    own_live = own_mask.astype(jnp.float32)
    x_own = jnp.transpose(x_points.reshape(dim_count, row_count, BS)[:, own_rows, :], (1, 0, 2))
    my_group = dp_index // owner_ratio
    my_part = dp_index % owner_ratio
    dest_rows = all_rows[:, ind_index, :]
    dest_cols = all_cols[:, ind_index, :]
    source_rows = all_rows[:, my_group, :]
    source_cols = all_cols[:, my_group, :]
    source_live = live_all[:, my_group, :]
    matched = source_live[:, None, :] & (source_rows[:, None, :] == dest_rows[:, :, None])
    found_col = jnp.sum(jnp.where(matched, source_cols[:, None, :], 0), axis=2)
    dest_live = live_all[:, ind_index, :]
    keep = jnp.any(matched, axis=2) & (found_col // own_blocks == my_part) & dest_live
    pick_rows = jnp.where(keep, found_col - my_part * own_blocks, 0)
    pick_cols = jnp.where(keep, dest_cols, 0)

    def pair_first(values):
        return jnp.transpose(
            values.reshape(groups_ind, owner_ratio, slot_count), (1, 0, 2)
        ).reshape(-1)

    outgoing = pick_tiles(
        dpsi_grad,
        pair_first(pick_rows),
        pair_first(pick_cols),
        pair_first(keep.astype(jnp.int32)),
    ).reshape(owner_ratio, groups_ind * slot_count, BS, BS)
    swap = [(index, index ^ 1) for index in range(groups_dp)]
    from_pair = lax.ppermute(outgoing[1 - my_part], "dp", swap)
    combined = (outgoing[my_part] + from_pair).reshape(groups_ind, slot_count, BS, BS)
    grouped = exchange(combined, "dp", 3, stride=owner_ratio, same=False, space=pl.ANY)
    row_tiles = all_rows[dp_index]
    col_tiles = all_cols[dp_index]
    live_tiles = live_all[dp_index]
    near_match = live_tiles[None, :, :] & (row_tiles[None, :, :] == own_rows[:, None, None])
    near_weight = jnp.any(near_match, axis=2).astype(jnp.float32)
    near_local = jnp.sum(jnp.where(near_match, col_tiles[None, :, :], 0), axis=2)
    group_ids = jnp.arange(groups_ind, dtype=jnp.int32)
    z_near = jnp.transpose(
        z_blocks[group_ids[None, :], :, near_local, :], (0, 2, 1, 3)
    ).reshape(slot_count, dim_count, groups_ind * BS)
    kernel, _ = batched_kernel(x_own, z_near, length_scales)
    masked = kernel * jnp.repeat(near_weight, BS, axis=1)[:, None, :]
    dk_local = jnp.einsum(
        "spgk,gskc->spc", masked.reshape(slot_count, BS, groups_ind, BS), grouped, precision=highest
    )
    dk_local = dk_local * own_live[:, None, None]
    z_own = jnp.transpose(z_points.reshape(dim_count, col_blocks, BS)[:, own_cols, :], (1, 0, 2))
    _, slopes = batched_kernel(x_own, z_own, length_scales)
    grad_k = dk_local * slopes
    col_sum = jnp.sum(grad_k, axis=1)
    x_weighted = jnp.einsum("sqn,snm->sqm", x_own, grad_k, precision=highest)
    inverse_square = -2.0 / (length_scales * length_scales)
    z_parts = inverse_square[None, :, None] * (x_weighted - z_own * col_sum[:, None, :])
    scale_terms = []
    for dim_q in range(dim_count):
        offset = x_own[:, dim_q, :, None] - z_own[:, dim_q, None, :]
        scale_terms.append(jnp.sum(grad_k * offset * offset, axis=(1, 2)))
    cube_scale = length_scales * length_scales * length_scales
    scale_parts = (-2.0 / cube_scale)[None, :] * jnp.stack(scale_terms, axis=1)
    part_rows = slot_count * dim_count
    scale_row = jnp.pad(jnp.sum(scale_parts, axis=0), (0, BS - dim_count))[None, :]
    sent = jnp.concatenate([z_parts.reshape(part_rows, BS), scale_row])
    sent = jnp.pad(sent, ((0, -(part_rows + 1) % 8), (0, 0)))
    parts = exchange(sent, "dp", 4)
    scale_sum = jnp.sum(parts[:, part_rows, :128], axis=0)
    scale_all = exchange(jnp.broadcast_to(scale_sum[None, :], (8, 128)), "ind", 5)
    scale_grad = jnp.sum(scale_all[:, 0, :dim_count], axis=0)
    onehot = (
        dest_cols.reshape(-1)[:, None] == jnp.arange(col_blocks, dtype=jnp.int32)[None, :]
    ).astype(jnp.float32)
    z_grad = jnp.einsum(
        "tc,tqb->qcb",
        onehot,
        parts[:, :part_rows, :].reshape(groups_dp * slot_count, dim_count, BS),
        precision=highest,
    ).reshape(dim_count, col_blocks * BS)
    return (dk_local.reshape(1, 1, slot_count, BS, BS), z_grad, scale_grad)


def solution(mesh):
    return jax.shard_map(
        on_device,
        mesh=mesh,
        in_specs=(
            P(None, "dp"),
            P(None, "ind"),
            P(),
            P("dp", "ind"),
            P("dp", "ind", None),
            P("dp", "ind", None),
            P("dp", "ind"),
        ),
        out_specs=(P("dp", "ind", None, None, None), P(None, "ind"), P()),
        check_vma=False,
    )
```

time: 607 us -> 192 us (0.32)
  blocking collectives: 248 us -> 0 us
  local copies, waits for them, and re-layouts: 189 us -> 19.2 us
  Pallas kernels: 0 us -> 134 us
  waiting for transfers between devices: 121 us -> 0.01 us
  other arithmetic: 19.3 us -> 12.3 us
    gather x145 -> x1, local copies, waits for them, and re-layouts: 186 us -> 1.71 us  [on_device(): z_blocks[group_ids[None, :], :, near_local, :]]
    all_gather x3 -> x0, blocking collectives: 150 us -> none  [the longest x1 69.5 us: on_device(): lax.all_gather(block_rows, ('dp', 'ind'), axis=0, tiled=True)]
    pallas_call x0 -> x7, Pallas kernels: none -> 134 us  [the longest x6 110 us: exchange(): pl.pallas_call(functools.partial(exchange_kernel, axis, stride, same), ou...]
    all_to_all x1 -> x0, waiting for transfers between devices: 121 us -> none  [on_device(): lax.all_to_all(outgoing, 'dp', split_axis=0, concat_axis=0, tiled=True)]
    psum x2 -> x0, blocking collectives: 61.5 us -> none  [the longest x1 37.2 us: on_device(): scale_grad = lax.psum(scale_local, ('dp', 'ind'))]
    unnamed x1 -> x0, blocking collectives: 36.8 us -> none
    mul x4 -> x0, other arithmetic: 11.4 us -> none  [the longest x1 11.3 us: pick_tile(): return lax.dynamic_slice(dpsi_grad, (row_at, col_at), (BS, BS)) * weight]
    add x0 -> x1, other arithmetic: none -> 8.24 us  [on_device(): outgoing[my_part] + from_pair]
  transfers between devices with their start and end apart: 1 -> 1, of which waited for: 1 -> 0; matrix products, arithmetic and copies ran while one was open for 1% -> 3% of each run, Pallas kernels for 0% -> 5%
where the time goes in v1:
time: 192 us; the launch traced here: 191 us
  Pallas kernels  134 us (70%)
  local copies, waits for them, and re-layouts  19.2 us (10%)
  matrix products  18.8 us (10%)
  other arithmetic  12.3 us (6%)
  starting transfers between devices  4.41 us (2%)
    pallas_call x6, Pallas kernels, exchange(): pl.pallas_call(functools.partial(exchange_kernel, axis, stride, same), ou...  110 us
    pallas_call x1, Pallas kernels, pick_tiles(): pl.pallas_call(pick_kernel, out_shape=jax.ShapeDtypeStruct((count, BS, BS...  24.7 us
    dot_general x1, matrix products, on_device(): jnp.einsum('spgk,gskc->spc', masked.reshape(slot_count, BS, groups_ind, B...  17.8 us
    add x1, other arithmetic, on_device(): outgoing[my_part] + from_pair  8.24 us
    squeeze x1, local copies, waits for them, and re-layouts, on_device(): from_pair = lax.ppermute(outgoing[1 - my_part], 'dp', swap)  6.01 us
    ppermute x1, starting transfers between devices, on_device(): from_pair = lax.ppermute(outgoing[1 - my_part], 'dp', swap)  4.41 us
  transfers between devices with their start and end apart: 1, of which 0 were waited for; matrix products, arithmetic and copies ran while one was open for 3% of the time, Pallas kernels for 5%

profile of v1, /device:TPU:0, one launch (start us, length us, event | category | flops | bytes accessed | tf_op | source)
XLA Modules:
  0.0 190.8 jit_solution(3011824808274996078)
XLA Ops:
  1.3 0.7 pad_bitcast_fusion.2
  2.0 0.7 pad_bitcast_fusion
  3.2 8.6 %shard_map.95 = s32[4,8,128]{2,1,0:T(8,128)} custom-call(s32[8,128]{1,0:T(8,128)} %pad.26.in_ref), custom_call_target="tpu_custom_call" | custom-call | tf_op jit(solution)/shard_map/pallas_call | solution.py:65
  11.8 6.7 %shard_map.96 = s32[8,32,128]{2,1,0:T(8,128)} custom-call(s32[32,128]{1,0:T(8,128)} %bitcast.132), custom_call_target="tpu_custom_call" | custom-call | tf_op jit(solution)/shard_map/pallas_call | solution.py:65
  18.6 1.0 fusion.72
  19.6 0.9 slice.91
  22.9 0.6 reshape.177.keep_ref
  23.5 24.7 %shard_map.97 = f32[48,256,256]{2,1,0:T(8,128)} custom-call(s32[48]{0:T(128)} %reshape.165.row_ref, s32[48]{0:T(128)} %reshape.166.col_ref, s32[48]{0:T(128)} %reshape.177.keep_ref, f32[2048,4096]{1,0:T(8,128)} %in_ref.3), custom_call_target="tpu_custom_call" | custom-call | tf_op jit(solution)/shard_map/pallas_call | solution.py:93
  48.2 6.0 %dynamic-slice_bitcast_fusion = f32[24,256,256]{2,1,0:T(8,128)} fusion(f32[2,24,256,256]{3,2,1,0:T(8,128)} %bitcast.123, s32[]{:T(128)S(6)} %select_n.139), kind=kLoop, calls=%fused_computation.9 | loop fusion | bytes 12582916 | tf_op jit(solution)/shard_map/squeeze | solution.py:168
  54.2 4.4 %collective-permute-start = (f32[24,256,256]{2,1,0:T(8,128)}, f32[24,256,256]{2,1,0:T(8,128)}, u32[]{:S(2)}, u32[]{:S(2)}) collective-permute-start(f32[24,256,256]{2,1,0:T(8,128)} %dynamic-slice_bitcast_fusion), channel_id=1, source_target_pairs={{0,4},{4,0},{8,12},{12,8},{16,20},{20,16},{24,28},{28,24},{1,5},{5... | collective-permute-start | bytes 18874376 | tf_op jit(solution)/shard_map/ppermute | solution.py:168
  59.3 10.0 %shard_map.94 = f32[4,3,4096]{2,1,0:T(4,128)} custom-call(f32[3,4096]{1,0:T(4,128)} %in_ref.2), custom_call_target="tpu_custom_call" | custom-call | tf_op jit(solution)/shard_map/pallas_call | solution.py:65
  69.4 1.7 gather_fusion.1
  71.6 1.4 gather_fusion.2
  74.3 8.2 %bitcast_add_fusion = f32[24,256,256]{2,1,0:T(8,128)} fusion(f32[24,256,256]{2,1,0:T(8,128)} %collective-permute-done, f32[2,24,256,256]{3,2,1,0:T(8,128)} %bitcast.124, s32[]{:T(128)S(6)} %select_n.138), kind=kLoop, calls=%fused_computation.7 | loop fusion | flops 1572864 | bytes 18874372 | tf_op jit(solution)/shard_map/add | solution.py:169
  82.6 69.7 %shard_map.98 = f32[4,6,256,256]{3,2,1,0:T(8,128)} custom-call(f32[4,6,256,256]{3,2,1,0:T(8,128)} %bitcast.125), custom_call_target="tpu_custom_call" | custom-call | tf_op jit(solution)/shard_map/pallas_call | solution.py:65
  152.3 17.8 %fusion.70 = (f32[6,256]{1,0:T(8,128)S(1)}, f32[6]{0:T(128)S(1)}, f32[6]{0:T(128)S(1)}, f32[6]{0:T(128)S(1)}, f32[6,256,256]{2,1,0:T(8,128)S(1)}, /*index=5*/f32[6,256,256]{2,1,0:T(8,128)}) fusion(f32[6,256]{1,0:T(8,128)S(1)} %bitcast.141, f32[6,256]{1,0:T(8,128)S(1)} %bitcast.144, f32[6,256]{1,0:T(8,128)S(1)} %bitcast.142, f32[6,256]{1,0:T(8,128)S(1)} %bitcast.145, ...), kind=kOutput, calls=%fused_computation.135 | convolution fusion | flops 4874304000 | bytes 9554124 | tf_op jit(solution)/shard_map/spgk,gskc->spc/dot_general | solution.py:183
  170.1 0.9 fusion.51
  171.2 0.6 select_maximum_fusion.in_ref
  171.8 7.3 %shard_map.99 = f32[8,24,256]{2,1,0:T(8,128)} custom-call(f32[24,256]{1,0:T(8,128)} %select_maximum_fusion.in_ref), custom_call_target="tpu_custom_call" | custom-call | tf_op jit(solution)/shard_map/pallas_call | solution.py:65
  179.1 0.8 slice_reduce_fusion
  179.8 1.0 reshape.174
  181.0 0.7 copy.60
  182.3 7.3 %shard_map.100 = f32[4,8,128]{2,1,0:T(8,128)} custom-call(f32[8,128]{1,0:T(8,128)} %broadcast_in_dim.92.in_ref), custom_call_target="tpu_custom_call" | custom-call | tf_op jit(solution)/shard_map/pallas_call | solution.py:65
  189.6 1.2 slice_reduce_fusion.1
  (72 shorter events, 6.2 us)
Async XLA Ops:
  0.6 72.4 %copy-start = (f32[3,2048]{1,0:T(4,128)S(1)}, f32[3,2048]{1,0:T(4,128)}, u32[]{:S(2)}) copy-start(f32[3,2048]{1,0:T(4,128)} %param.7) | copy-start | bytes 73732
  48.2 10.6 %copy-start.4 = (s32[1,1,6]{2,1,0:T(1,128)S(1)}, s32[1,1,6]{2,1,0:T(1,128)}, u32[]{:S(2)}) copy-start(s32[1,1,6]{2,1,0:T(1,128)} %param.11) | copy-start | bytes 76
  48.2 23.3 %copy-start.3 = (s32[1,1,6]{2,1,0:T(1,128)S(1)}, s32[1,1,6]{2,1,0:T(1,128)}, u32[]{:S(2)}) copy-start(s32[1,1,6]{2,1,0:T(1,128)} %param.12) | copy-start | bytes 76
  48.2 25.5 %copy-start.2 = (f32[3]{0:T(128)S(1)}, f32[3]{0:T(128)}, u32[]{:S(2)}) copy-start(f32[3]{0:T(128)} %param.9) | copy-start | bytes 40
  54.2 20.1 %collective-permute-start = (f32[24,256,256]{2,1,0:T(8,128)}, f32[24,256,256]{2,1,0:T(8,128)}, u32[]{:S(2)}, u32[]{:S(2)}) collective-permute-start(f32[24,256,256]{2,1,0:T(8,128)} %dynamic-slice_bitcast_fusion), channel_id=1, source_target_pairs={{0,4},{4,0},{8,12},{12,8},{16,20},{20,16},{24,28},{28,24},{1,5},{5... | collective-permute-start | bytes 18874376 | tf_op jit(solution)/shard_map/ppermute | solution.py:168
  152.3 38.5 %copy-start.1 = (f32[3,2048]{1,0:T(4,128)S(1)}, f32[3,2048]{1,0:T(4,128)}, u32[]{:S(2)}) copy-start(f32[3,2048]{1,0:T(4,128)} %param.7) | copy-start | bytes 73732

commit v2 on v1

--- a/solution.py
+++ b/solution.py
@@ -9,6 +9,7 @@
 
 M = 16384
 BS = 256
+PICKS = 4
 
 
 def wendland(x_rows, z_cols, length_scales):
@@ -76,30 +77,45 @@
     )(array)
 
 
-def pick_kernel(row_ref, col_ref, keep_ref, in_ref, out_ref):
-    keep = keep_ref[pl.program_id(0)] > 0
-
-    @pl.when(keep)
-    def _():
-        out_ref[0] = in_ref[...]
-
-    @pl.when(jnp.logical_not(keep))
-    def _():
-        out_ref[...] = jnp.zeros_like(out_ref)
-
-
-def pick_tiles(dpsi_grad, row_blocks, col_blocks, keep):
+def pick_kernel(has_other, row_ref, col_ref, keep_ref, *refs):
+    out_ref = refs[-1]
+    for place in range(PICKS):
+        keep = keep_ref[pl.program_id(0) * PICKS + place] > 0
+
+        @pl.when(keep)
+        def _():
+            out_ref[place] = refs[place][...]
+
+        @pl.when(jnp.logical_not(keep))
+        def _():
+            if has_other:
+                out_ref[place] = refs[PICKS][place]
+            else:
+                out_ref[place] = jnp.zeros_like(out_ref[place])
+
+
+def pick_tiles(dpsi_grad, row_blocks, col_blocks, keep, other=None):
     count = row_blocks.shape[0]
+    stacked = pl.BlockSpec((PICKS, BS, BS), lambda t, rows, cols, keeps: (t, 0, 0))
+
+    def tile_spec(place):
+        return pl.BlockSpec(
+            (BS, BS),
+            lambda t, rows, cols, keeps: (rows[t * PICKS + place], cols[t * PICKS + place]),
+        )
+
+    extra = [] if other is None else [other]
     return pl.pallas_call(
-        pick_kernel,
+        functools.partial(pick_kernel, other is not None),
         out_shape=jax.ShapeDtypeStruct((count, BS, BS), dpsi_grad.dtype),
         grid_spec=pltpu.PrefetchScalarGridSpec(
             num_scalar_prefetch=3,
-            grid=(count,),
-            in_specs=[pl.BlockSpec((BS, BS), lambda t, rows, cols, keeps: (rows[t], cols[t]))],
-            out_specs=pl.BlockSpec((1, BS, BS), lambda t, rows, cols, keeps: (t, 0, 0)),
+            grid=(count // PICKS,),
+            in_specs=[tile_spec(place) for place in range(PICKS)] + [stacked] * len(extra),
+            out_specs=stacked,
         ),
-    )(row_blocks, col_blocks, keep, dpsi_grad)
+        compiler_params=pltpu.CompilerParams(vmem_limit_bytes=24 * 1024 * 1024),
+    )(row_blocks, col_blocks, keep, *([dpsi_grad] * PICKS), *extra)
 
 
 def on_device(x_points, z_points, length_scales, dpsi_grad, block_rows, block_cols, block_count):
@@ -156,17 +172,14 @@
     def pair_first(values):
         return jnp.transpose(
             values.reshape(groups_ind, owner_ratio, slot_count), (1, 0, 2)
-        ).reshape(-1)
-
-    outgoing = pick_tiles(
-        dpsi_grad,
-        pair_first(pick_rows),
-        pair_first(pick_cols),
-        pair_first(keep.astype(jnp.int32)),
-    ).reshape(owner_ratio, groups_ind * slot_count, BS, BS)
+        ).reshape(owner_ratio, -1)
+
+    pick_lists = (pair_first(pick_rows), pair_first(pick_cols), pair_first(keep.astype(jnp.int32)))
+    outgoing = pick_tiles(dpsi_grad, *[values[1 - my_part] for values in pick_lists])
     swap = [(index, index ^ 1) for index in range(groups_dp)]
-    from_pair = lax.ppermute(outgoing[1 - my_part], "dp", swap)
-    combined = (outgoing[my_part] + from_pair).reshape(groups_ind, slot_count, BS, BS)
+    from_pair = lax.ppermute(outgoing, "dp", swap)
+    combined = pick_tiles(dpsi_grad, *[values[my_part] for values in pick_lists], from_pair)
+    combined = combined.reshape(groups_ind, slot_count, BS, BS)
     grouped = exchange(combined, "dp", 3, stride=owner_ratio, same=False, space=pl.ANY)
     row_tiles = all_rows[dp_index]
     col_tiles = all_cols[dp_index]

time: 192 us -> 165 us (0.86)
  Pallas kernels: 134 us -> 124 us
  other arithmetic: 12.3 us -> 4.08 us
  local copies, waits for them, and re-layouts: 19.2 us -> 14.3 us
  starting transfers between devices: 4.41 us -> 0.51 us
    pallas_call x1 -> x2, Pallas kernels: 24.7 us -> 12.9 us  [pick_tiles(): pl.pallas_call(functools.partial(pick_kernel, other is not None), out_sha...]
    add x1 -> x0, other arithmetic: 8.24 us -> none  [on_device(): outgoing[my_part] + from_pair]
    squeeze x1 -> x3, local copies, waits for them, and re-layouts: 6.01 us -> 0.02 us  [on_device(): values[1 - my_part]]
    ppermute x1, starting transfers between devices: 4.41 us -> 0.51 us  [on_device(): from_pair = lax.ppermute(outgoing, 'dp', swap)]
    unnamed x19, local copies, waits for them, and re-layouts: 0.82 us -> 3.47 us
    pallas_call x6, Pallas kernels: 110 us -> 112 us  [exchange(): pl.pallas_call(functools.partial(exchange_kernel, axis, stride, same), ou...]
  transfers between devices with their start and end apart: 1 -> 1, of which waited for: 0 -> 0; matrix products, arithmetic and copies ran while one was open for 3% -> 3% of each run, Pallas kernels for 5% -> 7%
where the time goes in v2:
time: 165 us; the launch traced here: 164 us
  Pallas kernels  124 us (75%)
  matrix products  18.9 us (11%)
  local copies, waits for them, and re-layouts  14.3 us (9%)
  other arithmetic  4.08 us (2%)
  between operations  1.7 us (1%)
    pallas_call x6, Pallas kernels, exchange(): pl.pallas_call(functools.partial(exchange_kernel, axis, stride, same), ou...  112 us
    dot_general x1, matrix products, on_device(): jnp.einsum('spgk,gskc->spc', masked.reshape(slot_count, BS, groups_ind, B...  17.8 us
    pallas_call x2, Pallas kernels, pick_tiles(): pl.pallas_call(functools.partial(pick_kernel, other is not None), out_sha...  12.9 us
    unnamed x19, local copies, waits for them, and re-layouts  3.47 us
  transfers between devices with their start and end apart: 1, of which 0 were waited for; matrix products, arithmetic and copies ran while one was open for 3% of the time, Pallas kernels for 7%

profile of v2, /device:TPU:0, one launch (start us, length us, event | category | flops | bytes accessed | tf_op | source)
XLA Modules:
  0.0 163.9 jit_solution(13174335070768401237)
XLA Ops:
  1.3 0.7 pad_bitcast_fusion.2
  2.0 0.7 pad_bitcast_fusion
  2.6 0.6 pad.26.in_ref
  3.2 8.6 %shard_map.95 = s32[4,8,128]{2,1,0:T(8,128)} custom-call(s32[8,128]{1,0:T(8,128)} %pad.26.in_ref), custom_call_target="tpu_custom_call" | custom-call | tf_op jit(solution)/shard_map/pallas_call | solution.py:66
  11.8 6.7 %shard_map.96 = s32[8,32,128]{2,1,0:T(8,128)} custom-call(s32[32,128]{1,0:T(8,128)} %bitcast.137), custom_call_target="tpu_custom_call" | custom-call | tf_op jit(solution)/shard_map/pallas_call | solution.py:66
  18.6 1.0 fusion.78
  19.6 0.9 slice.91
  22.0 6.6 %shard_map.97 = f32[24,256,256]{2,1,0:T(8,128)} custom-call(s32[24]{0:T(128)S(1)} %get-tuple-element.35.row_ref, s32[24]{0:T(128)S(1)} %get-tuple-element.33.col_ref, s32[24]{0:T(128)S(1)} %get-tuple-element.31.keep_ref, f32[2048,4096]{1,0:T(8,128)} %refs_3_.3, f32[2048,4096]{1,0:T(8,128)} %refs_3_.3, f32[2048,4096]{1,0:T(8,128)} %refs_3_.3, ...), custom_call_target="tpu_custom_call" | custom-call | tf_op jit(solution)/shard_map/pallas_call | solution.py:108
  29.8 10.7 %shard_map.94 = f32[4,3,4096]{2,1,0:T(4,128)} custom-call(f32[3,4096]{1,0:T(4,128)} %in_ref.1), custom_call_target="tpu_custom_call" | custom-call | tf_op jit(solution)/shard_map/pallas_call | solution.py:66
  40.5 1.7 %gather_fusion.1 = f32[24,3,256]{2,1,0:T(4,128)S(1)} fusion(f32[4,3,16,256]{3,1,2,0:T(4,128)} %bitcast.132, s32[24]{0:T(128)S(1)} %reshape.184), kind=kCustom, calls=%fused_computation.1 | custom fusion | bytes 147648 | tf_op jit(solution)/shard_map/gather | solution.py:192
  42.7 1.4 gather_fusion.2
  44.8 0.6 fusion.82
  45.5 6.3 %shard_map.98 = f32[24,256,256]{2,1,0:T(8,128)S(1)} custom-call(s32[24]{0:T(128)S(1)} %get-tuple-element.36.row_ref, s32[24]{0:T(128)S(1)} %get-tuple-element.34.col_ref, s32[24]{0:T(128)S(1)} %get-tuple-element.32.keep_ref, f32[2048,4096]{1,0:T(8,128)} %refs_3_.3, f32[2048,4096]{1,0:T(8,128)} %refs_3_.3, f32[2048,4096]{1,0:T(8,128)} %refs_3_.3, ...), custom_call_target="tpu_custom_call" | custom-call | tf_op jit(solution)/shard_map/pallas_call | solution.py:108
  51.8 2.6 %copy-done.1 = f32[24,256,256]{2,1,0:T(8,128)} copy-done((f32[24,256,256]{2,1,0:T(8,128)}, f32[24,256,256]{2,1,0:T(8,128)S(1)}, u32[]{:S(2)}) %copy-start.1) | copy-done | bytes 6291480
  54.4 71.0 %shard_map.99 = f32[4,6,256,256]{3,2,1,0:T(8,128)} custom-call(f32[4,6,256,256]{3,2,1,0:T(8,128)} %bitcast.130), custom_call_target="tpu_custom_call" | custom-call | tf_op jit(solution)/shard_map/pallas_call | solution.py:66
  125.4 17.8 %fusion.76 = (f32[6,256]{1,0:T(8,128)S(1)}, f32[6]{0:T(128)S(1)}, f32[6]{0:T(128)S(1)}, f32[6]{0:T(128)S(1)}, f32[6,256,256]{2,1,0:T(8,128)S(1)}, /*index=5*/f32[6,256,256]{2,1,0:T(8,128)}) fusion(f32[6,256]{1,0:T(8,128)S(1)} %bitcast.146, f32[6,256]{1,0:T(8,128)S(1)} %bitcast.149, f32[6,256]{1,0:T(8,128)S(1)} %bitcast.147, f32[6,256]{1,0:T(8,128)S(1)} %bitcast.150, ...), kind=kOutput, calls=%fused_computation.145 | convolution fusion | flops 4874304000 | bytes 9554124 | tf_op jit(solution)/shard_map/spgk,gskc->spc/dot_general | solution.py:196
  143.2 0.9 fusion.51
  144.3 0.6 select_maximum_fusion.in_ref
  144.9 7.1 %shard_map.100 = f32[8,24,256]{2,1,0:T(8,128)} custom-call(f32[24,256]{1,0:T(8,128)} %select_maximum_fusion.in_ref), custom_call_target="tpu_custom_call" | custom-call | tf_op jit(solution)/shard_map/pallas_call | solution.py:66
  152.1 0.8 slice_reduce_fusion
  152.8 1.0 reshape.171
  154.0 0.7 copy.60
  155.3 7.4 %shard_map.101 = f32[4,8,128]{2,1,0:T(8,128)} custom-call(f32[8,128]{1,0:T(8,128)} %broadcast_in_dim.92.in_ref), custom_call_target="tpu_custom_call" | custom-call | tf_op jit(solution)/shard_map/pallas_call | solution.py:66
  162.7 1.2 slice_reduce_fusion.1
  (74 shorter events, 4.6 us)
Async XLA Ops:
  0.6 43.5 %copy-start = (f32[3,2048]{1,0:T(4,128)S(1)}, f32[3,2048]{1,0:T(4,128)}, u32[]{:S(2)}) copy-start(f32[3,2048]{1,0:T(4,128)} %param.7) | copy-start | bytes 73732
  22.0 7.3 %copy-start.4 = (s32[1,1,6]{2,1,0:T(1,128)S(1)}, s32[1,1,6]{2,1,0:T(1,128)}, u32[]{:S(2)}) copy-start(s32[1,1,6]{2,1,0:T(1,128)} %param.11) | copy-start | bytes 76
  22.0 20.7 %copy-start.3 = (s32[1,1,6]{2,1,0:T(1,128)S(1)}, s32[1,1,6]{2,1,0:T(1,128)}, u32[]{:S(2)}) copy-start(s32[1,1,6]{2,1,0:T(1,128)} %param.12) | copy-start | bytes 76
  22.0 22.8 %copy-start.2 = (f32[3]{0:T(128)S(1)}, f32[3]{0:T(128)}, u32[]{:S(2)}) copy-start(f32[3]{0:T(128)} %param.9) | copy-start | bytes 40
  28.6 16.9 %collective-permute-start = (f32[24,256,256]{2,1,0:T(8,128)}, f32[24,256,256]{2,1,0:T(8,128)}, u32[]{:S(2)}, u32[]{:S(2)}) collective-permute-start(f32[24,256,256]{2,1,0:T(8,128)} %shard_map.97), channel_id=1, source_target_pairs={{0,4},{4,0},{8,12},{12,8},{16,20},{20,16},{24,28},{28,24},{1,5},{5... | collective-permute-start | bytes 18874376 | tf_op jit(solution)/shard_map/ppermute | solution.py:180
  51.7 2.7 %copy-start.1 = (f32[24,256,256]{2,1,0:T(8,128)}, f32[24,256,256]{2,1,0:T(8,128)S(1)}, u32[]{:S(2)}) copy-start(f32[24,256,256]{2,1,0:T(8,128)S(1)} %shard_map.98) | copy-start | bytes 18874372
